TPU v7x, 128 devices: a whole 4x4x4 slice. The times are simulated.
128 devices in a mesh: dp: 16 (over z, x), seq: 8 (over y, core).
Axes of the slice: x: 4, y: 4, z: 4, core: 2. Of those that a mesh axis runs over, the one named last changes fastest.
Arguments:
- queries: bfloat16 [16384, 4096], P(('dp', 'seq')), may hold values from -6 to 6
- keys: bfloat16 [16384, 4096], P(('dp', 'seq')), may hold values from -6 to 6
- values: bfloat16 [16384, 4096], P(('dp', 'seq')), may hold values from -6 to 6
- grad_mixed: bfloat16 [16384, 4096], P(('dp', 'seq')), may hold values from -6 to 6
- doc_lengths: int32 [16, 8], replicated, may hold values from 1 to 512, 1024 in all within a row
- owner: int32 [16], replicated, may hold values from 0 to 15, each once
Outputs:
- mixed: bfloat16 [16384, 4096], P(('dp', 'seq'))
- grad_queries: bfloat16 [16384, 4096], P(('dp', 'seq'))
- grad_keys: bfloat16 [16384, 4096], P(('dp', 'seq'))
- grad_values: bfloat16 [16384, 4096], P(('dp', 'seq'))
Inputs may be any that keep to these rules, and one draw needn't show every extreme that they name: `doc_lengths`: each row holds positive lengths that sum to 1024, the largest exactly 512. `owner`: a permutation of the data groups.
All inputs are finite; a program needn't handle non-finite values.
Results may differ from a plain program's by a relative error of at most 0.012.
Values may be sent and summed in bfloat16 or wider, within the bound.
No kernel may reach another device: no remote copies, remote signals or barrier semaphores. Data moves between devices by JAX's collectives and lax.ppermute only.
A program may use at most 128 MiB of HBM per device.

v0:
```python
import jax
import jax.numpy as jnp
from jax import lax
from jax.sharding import PartitionSpec as P

HEAD_TOTAL = 32


def doc_ids(lengths, count):
    ends = jnp.cumsum(lengths)
    places = jnp.arange(count, dtype=jnp.int32)
    return jnp.sum((places[:, None] >= ends[None, :]).astype(jnp.int32), axis=1)


def head_grads(query, key_rows, value_rows, cotangent, doc):
    count = query.shape[0]
    places = jnp.arange(count, dtype=jnp.int32)
    allowed = (places[None, :] < places[:, None]) & (doc[:, None] == doc[None, :])
    scale = query.shape[1] ** (-0.5)

    def forward(qa, ka, va):
        scores = jnp.dot(qa, ka.T, preferred_element_type=jnp.float32) * scale
        spent = jnp.where(allowed, jax.nn.softplus(scores), 0.0)
        rest = lax.cumsum(spent, axis=1, reverse=True) - spent
        weight = jnp.where(allowed, jnp.exp(jax.nn.log_sigmoid(scores) - rest), 0.0)
        return jnp.dot(weight.astype(jnp.bfloat16), va, preferred_element_type=jnp.float32)

    out, pull = jax.vjp(forward, query, key_rows, value_rows)
    grad_q, grad_k, grad_v = pull(cotangent.astype(jnp.float32))
    return (out.astype(jnp.bfloat16), grad_q, grad_k, grad_v)


def local(queries, keys, values, grad_mixed, doc_lengths, owner):
    rows, width = queries.shape
    head_count = HEAD_TOTAL
    head_size = width // head_count
    group = lax.axis_index("dp")
    groups = lax.axis_size("dp")

    def split(x):
        return x.reshape(rows, head_count, head_size)

    qh, kh, vh, gh = (
        lax.all_to_all(split(queries), "seq", split_axis=1, concat_axis=0, tiled=True),
        lax.all_to_all(split(keys), "seq", split_axis=1, concat_axis=0, tiled=True),
        lax.all_to_all(split(values), "seq", split_axis=1, concat_axis=0, tiled=True),
        lax.all_to_all(split(grad_mixed), "seq", split_axis=1, concat_axis=0, tiled=True),
    )
    length_row = lax.dynamic_index_in_dim(doc_lengths, group, 0, keepdims=False)
    doc = doc_ids(length_row, qh.shape[0])

    def by_head(x):
        return jnp.moveaxis(x, 1, 0)

    results = lax.map(
        lambda t: head_grads(t[0], t[1], t[2], t[3], doc),
        (by_head(qh), by_head(kh), by_head(vh), by_head(gh)),
    )
    out_h, gq_h, gk_h, gv_h = [jnp.moveaxis(x, 0, 1) for x in results]
    out_r, gq_r, gk_r, gv_r = (
        lax.all_to_all(out_h, "seq", split_axis=0, concat_axis=1, tiled=True),
        lax.all_to_all(gq_h, "seq", split_axis=0, concat_axis=1, tiled=True),
        lax.all_to_all(gk_h, "seq", split_axis=0, concat_axis=1, tiled=True),
        lax.all_to_all(gv_h, "seq", split_axis=0, concat_axis=1, tiled=True),
    )
    out_rows = out_r.reshape(rows, width)
    target = lax.dynamic_index_in_dim(owner, group, 0, keepdims=False)
    onehot = (jnp.arange(groups, dtype=jnp.int32) == target).astype(jnp.bfloat16)
    slots = (onehot[:, None, None] * out_rows[None]).reshape(groups * rows, width)
    landed = lax.all_to_all(slots, "dp", split_axis=0, concat_axis=0, tiled=True)
    mixed = jnp.sum(landed.reshape(groups, rows, width).astype(jnp.float32), axis=0).astype(
        jnp.bfloat16
    )
    return (mixed, gq_r.reshape(rows, width), gk_r.reshape(rows, width), gv_r.reshape(rows, width))


def solution(mesh):
    placed = (
        P(("dp", "seq"), None),
        P(("dp", "seq"), None),
        P(("dp", "seq"), None),
        P(("dp", "seq"), None),
        P(),
        P(),
    )
    return jax.shard_map(
        local,
        mesh=mesh,
        in_specs=placed,
        out_specs=(
            P(("dp", "seq"), None),
            P(("dp", "seq"), None),
            P(("dp", "seq"), None),
            P(("dp", "seq"), None),
        ),
        check_vma=False,
    )
```

profile of v0, /device:TPU:1, one launch (start us, length us, event | category | flops | bytes accessed | tf_op | source)
XLA Modules:
  0.0 682.6 jit_solution(16968773300099775768)
XLA Ops:
  10.4 13.8 %all-to-all-done = bf16[128,32,128]{0,2,1:T(8,128)(2,1)S(1)} async-done(((bf16[128,32,128]{0,2,1:T(8,128)(2,1)}), bf16[128,32,128]{0,2,1:T(8,128)(2,1)S(1)}, u32[]{:S(2)}, u32[]{:S(2)}) %all-to-all-start) | async-done | bytes 1048608 | tf_op jit(solution)/shard_map/all_to_all | solution.py:44
  29.8 13.8 %all-to-all-done.1 = bf16[128,32,128]{0,2,1:T(8,128)(2,1)S(1)} async-done(((bf16[128,32,128]{0,2,1:T(8,128)(2,1)}), bf16[128,32,128]{0,2,1:T(8,128)(2,1)S(1)}, u32[]{:S(2)}, u32[]{:S(2)}) %all-to-all-start.1) | async-done | bytes 1048608 | tf_op jit(solution)/shard_map/all_to_all | solution.py:45
  50.2 12.8 %all-to-all-done.2 = bf16[128,32,128]{0,2,1:T(8,128)(2,1)S(1)} async-done(((bf16[128,32,128]{0,2,1:T(8,128)(2,1)}), bf16[128,32,128]{0,2,1:T(8,128)(2,1)S(1)}, u32[]{:S(2)}, u32[]{:S(2)}) %all-to-all-start.2) | async-done | bytes 1048608 | tf_op jit(solution)/shard_map/all_to_all | solution.py:46
  71.8 11.4 %all-to-all-done.3 = bf16[128,32,128]{0,2,1:T(8,128)(2,1)} async-done(((bf16[128,32,128]{0,2,1:T(8,128)(2,1)}), bf16[128,32,128]{0,2,1:T(8,128)(2,1)}, u32[]{:S(2)}, u32[]{:S(2)}) %all-to-all-start.3) | async-done | bytes 1048608 | tf_op jit(solution)/shard_map/all_to_all | solution.py:47
  85.6 250.0 %while.16 = (s32[]{:T(128)}, bf16[4,1024,128]{2,1,0:T(8,128)(2,1)}, bf16[4,1024,128]{2,1,0:T(8,128)(2,1)}, bf16[4,1024,128]{2,1,0:T(8,128)(2,1)}, bf16[4,1024,12...) while((s32[]{:T(128)}, bf16[4,1024,128]{2,1,0:T(8,128)(2,1)}, ...), condition=%wide.region_7.8_spmd, body=%wide.region_2.7_spmd.sunk | while | flops 1967519744 | bytes 207079792 | solution.py:55
  91.6 10.1 %fusion.81 = f32[1024,8,128]{0,1,2:T(8,128)S(1)} fusion(f32[1024,8,128]{0,2,1:T(8,128)S(1)} %bitcast.160), kind=kOutput, calls=%fused_computation.22.clone.1 | output fusion | flops 133169152 | bytes 8388608 | tf_op jit(solution)/shard_map/reduce-window
  109.0 9.5 %fusion.82 = (f32[1024,1024]{0,1:T(8,128)S(1)}, f32[1024,1024]{0,1:T(8,128)}, bf16[1024,1024]{0,1:T(8,128)(2,1)S(1)}) fusion(s32[1024]{0:T(1024)S(1)} %get-tuple-element.188, f32[1024,8,128]{0,2,1:T(8,128)S(1)} %copy.120, f32[1024,1024]{0,1:T(8,128)S(1)} %copy-done.4, bf16[4,1024,128]{2,1,0:T(8,128)(2,1)S(1)} %copy-done.11, s32[]{:T(128)S(6)} %copy.131, ...), kind=kOutput, calls=%fused_computation.30.clone.2 | convolution fusion | flops 295698432 | bytes 19407872 | tf_op jit(solution)/shard_map/while/body/eval_jaxpr/transpose(jvp())/dot_general | solution.py:26
  129.2 10.1 %fusion.85 = bf16[1024,1024]{0,1:T(8,128)(2,1)S(1)} fusion(f32[1024,8,128]{0,2,1:T(8,128)S(1)} %copy.121, f32[1024,1024]{0,1:T(8,128)S(1)} %copy-done.5, f32[1024,1024]{0,1:T(8,128)S(1)} %copy-done.6, bf16[1024,1024]{0,1:T(8,128)(2,1)S(1)} %get-tuple-element.158, s32[1024]{0:T(1024)S(1)} %get-tuple-element.188), kind=kLoop, calls=%fused_computation.11.clone.1 | loop fusion | flops 40894464 | bytes 16781312 | tf_op jit(solution)/shard_map/while/body/eval_jaxpr/transpose(jvp())/mul | solution.py:22
  148.1 6.1 fusion.80
  154.1 10.1 %fusion.81 = f32[1024,8,128]{0,1,2:T(8,128)S(1)} fusion(f32[1024,8,128]{0,2,1:T(8,128)S(1)} %bitcast.160), kind=kOutput, calls=%fused_computation.22.clone.1 | output fusion | flops 133169152 | bytes 8388608 | tf_op jit(solution)/shard_map/reduce-window
  171.5 9.5 %fusion.82 = (f32[1024,1024]{0,1:T(8,128)S(1)}, f32[1024,1024]{0,1:T(8,128)}, bf16[1024,1024]{0,1:T(8,128)(2,1)S(1)}) fusion(s32[1024]{0:T(1024)S(1)} %get-tuple-element.188, f32[1024,8,128]{0,2,1:T(8,128)S(1)} %copy.120, f32[1024,1024]{0,1:T(8,128)S(1)} %copy-done.4, bf16[4,1024,128]{2,1,0:T(8,128)(2,1)S(1)} %copy-done.11, s32[]{:T(128)S(6)} %copy.131, ...), kind=kOutput, calls=%fused_computation.30.clone.2 | convolution fusion | flops 295698432 | bytes 19407872 | tf_op jit(solution)/shard_map/while/body/eval_jaxpr/transpose(jvp())/dot_general | solution.py:26
  191.7 10.1 %fusion.85 = bf16[1024,1024]{0,1:T(8,128)(2,1)S(1)} fusion(f32[1024,8,128]{0,2,1:T(8,128)S(1)} %copy.121, f32[1024,1024]{0,1:T(8,128)S(1)} %copy-done.5, f32[1024,1024]{0,1:T(8,128)S(1)} %copy-done.6, bf16[1024,1024]{0,1:T(8,128)(2,1)S(1)} %get-tuple-element.158, s32[1024]{0:T(1024)S(1)} %get-tuple-element.188), kind=kLoop, calls=%fused_computation.11.clone.1 | loop fusion | flops 40894464 | bytes 16781312 | tf_op jit(solution)/shard_map/while/body/eval_jaxpr/transpose(jvp())/mul | solution.py:22
  216.6 10.1 %fusion.81 = f32[1024,8,128]{0,1,2:T(8,128)S(1)} fusion(f32[1024,8,128]{0,2,1:T(8,128)S(1)} %bitcast.160), kind=kOutput, calls=%fused_computation.22.clone.1 | output fusion | flops 133169152 | bytes 8388608 | tf_op jit(solution)/shard_map/reduce-window
  234.0 9.5 %fusion.82 = (f32[1024,1024]{0,1:T(8,128)S(1)}, f32[1024,1024]{0,1:T(8,128)}, bf16[1024,1024]{0,1:T(8,128)(2,1)S(1)}) fusion(s32[1024]{0:T(1024)S(1)} %get-tuple-element.188, f32[1024,8,128]{0,2,1:T(8,128)S(1)} %copy.120, f32[1024,1024]{0,1:T(8,128)S(1)} %copy-done.4, bf16[4,1024,128]{2,1,0:T(8,128)(2,1)S(1)} %copy-done.11, s32[]{:T(128)S(6)} %copy.131, ...), kind=kOutput, calls=%fused_computation.30.clone.2 | convolution fusion | flops 295698432 | bytes 19407872 | tf_op jit(solution)/shard_map/while/body/eval_jaxpr/transpose(jvp())/dot_general | solution.py:26
  254.2 10.1 %fusion.85 = bf16[1024,1024]{0,1:T(8,128)(2,1)S(1)} fusion(f32[1024,8,128]{0,2,1:T(8,128)S(1)} %copy.121, f32[1024,1024]{0,1:T(8,128)S(1)} %copy-done.5, f32[1024,1024]{0,1:T(8,128)S(1)} %copy-done.6, bf16[1024,1024]{0,1:T(8,128)(2,1)S(1)} %get-tuple-element.158, s32[1024]{0:T(1024)S(1)} %get-tuple-element.188), kind=kLoop, calls=%fused_computation.11.clone.1 | loop fusion | flops 40894464 | bytes 16781312 | tf_op jit(solution)/shard_map/while/body/eval_jaxpr/transpose(jvp())/mul | solution.py:22
  279.2 10.1 %fusion.81 = f32[1024,8,128]{0,1,2:T(8,128)S(1)} fusion(f32[1024,8,128]{0,2,1:T(8,128)S(1)} %bitcast.160), kind=kOutput, calls=%fused_computation.22.clone.1 | output fusion | flops 133169152 | bytes 8388608 | tf_op jit(solution)/shard_map/reduce-window
  296.5 9.5 %fusion.82 = (f32[1024,1024]{0,1:T(8,128)S(1)}, f32[1024,1024]{0,1:T(8,128)}, bf16[1024,1024]{0,1:T(8,128)(2,1)S(1)}) fusion(s32[1024]{0:T(1024)S(1)} %get-tuple-element.188, f32[1024,8,128]{0,2,1:T(8,128)S(1)} %copy.120, f32[1024,1024]{0,1:T(8,128)S(1)} %copy-done.4, bf16[4,1024,128]{2,1,0:T(8,128)(2,1)S(1)} %copy-done.11, s32[]{:T(128)S(6)} %copy.131, ...), kind=kOutput, calls=%fused_computation.30.clone.2 | convolution fusion | flops 295698432 | bytes 19407872 | tf_op jit(solution)/shard_map/while/body/eval_jaxpr/transpose(jvp())/dot_general | solution.py:26
  316.7 10.1 %fusion.85 = bf16[1024,1024]{0,1:T(8,128)(2,1)S(1)} fusion(f32[1024,8,128]{0,2,1:T(8,128)S(1)} %copy.121, f32[1024,1024]{0,1:T(8,128)S(1)} %copy-done.5, f32[1024,1024]{0,1:T(8,128)S(1)} %copy-done.6, bf16[1024,1024]{0,1:T(8,128)(2,1)S(1)} %get-tuple-element.158, s32[1024]{0:T(1024)S(1)} %get-tuple-element.188), kind=kLoop, calls=%fused_computation.11.clone.1 | loop fusion | flops 40894464 | bytes 16781312 | tf_op jit(solution)/shard_map/while/body/eval_jaxpr/transpose(jvp())/mul | solution.py:22
  344.9 13.3 %all-to-all-done.8 = bf16[1024,4,128]{2,1,0:T(4,128)(2,1)S(1)} async-done(((bf16[1024,4,128]{2,1,0:T(4,128)(2,1)}), bf16[1024,4,128]{2,1,0:T(4,128)(2,1)S(1)}, u32[]{:S(2)}, u32[]{:S(2)}) %all-to-all-start.8) | async-done | bytes 1048608 | tf_op jit(solution)/shard_map/all_to_all | solution.py:64
  364.3 13.3 %all-to-all-done.4 = bf16[1024,4,128]{2,1,0:T(4,128)(2,1)S(1)} async-done(((bf16[1024,4,128]{2,1,0:T(4,128)(2,1)}), bf16[1024,4,128]{2,1,0:T(4,128)(2,1)S(1)}, u32[]{:S(2)}, u32[]{:S(2)}) %all-to-all-start.4) | async-done | bytes 1048608 | tf_op jit(solution)/shard_map/all_to_all | solution.py:61
  408.0 9.3 %all-to-all-done.7 = bf16[1024,4,128]{2,1,0:T(4,128)(2,1)} async-done(((bf16[1024,4,128]{2,1,0:T(4,128)(2,1)}), bf16[1024,4,128]{2,1,0:T(4,128)(2,1)}, u32[]{:S(2)}, u32[]{:S(2)}) %all-to-all-start.7) | async-done | bytes 1048608 | tf_op jit(solution)/shard_map/all_to_all | solution.py:63
  417.3 7.7 %all-to-all-start.5 = ((bf16[16,128,4096]{2,1,0:T(8,128)(2,1)}), bf16[16,128,4096]{2,1,0:T(8,128)(2,1)}, u32[]{:S(2)}, u32[]{:S(2)}) async-start(bf16[16,128,4096]{2,1,0:T(8,128)(2,1)} %broadcast_multiply_fusion), calls=%async_computation.5 | async-start | bytes 33554432 | tf_op jit(solution)/shard_map/all_to_all | solution.py:70
  432.1 240.6 %all-to-all-done.5 = bf16[16,128,4096]{2,1,0:T(8,128)(2,1)} async-done(((bf16[16,128,4096]{2,1,0:T(8,128)(2,1)}), bf16[16,128,4096]{2,1,0:T(8,128)(2,1)}, u32[]{:S(2)}, u32[]{:S(2)}) %all-to-all-start.5) | async-done | bytes 16777248 | tf_op jit(solution)/shard_map/all_to_all | solution.py:70
  672.7 9.9 %reduce_sum.22 = bf16[128,4096]{1,0:T(8,128)(2,1)} reduce(bf16[16,128,4096]{2,1,0:T(8,128)(2,1)} %all-to-all-done.5, bf16[]{:T(256)} %constant.60.clone.1), dimensions={0}, to_apply=%region_8.9 | reduce | flops 7864320 | bytes 17825794 | tf_op jit(solution)/shard_map/reduce_sum | solution.py:71
  (181 shorter events, 210.8 us)
Async XLA Ops:
  0.6 67.4 %copy-start = (s32[16,8]{0,1:T(8,128)S(1)}, s32[16,8]{0,1:T(8,128)}, u32[]{:S(2)}) copy-start(s32[16,8]{0,1:T(8,128)} %param.12) | copy-start | bytes 1540
  0.6 8.4 %copy-start.7 = (bf16[128,4096]{1,0:T(8,128)(2,1)S(1)}, bf16[128,4096]{1,0:T(8,128)(2,1)}, u32[]{:S(2)}) copy-start(bf16[128,4096]{1,0:T(8,128)(2,1)} %param.9) | copy-start | bytes 3145732
  0.7 27.8 %copy-start.8 = (bf16[128,4096]{1,0:T(8,128)(2,1)S(1)}, bf16[128,4096]{1,0:T(8,128)(2,1)}, u32[]{:S(2)}) copy-start(bf16[128,4096]{1,0:T(8,128)(2,1)} %param.10) | copy-start | bytes 3145732
  3.1 21.1 %all-to-all-start = ((bf16[128,32,128]{0,2,1:T(8,128)(2,1)}), bf16[128,32,128]{0,2,1:T(8,128)(2,1)S(1)}, u32[]{:S(2)}, u32[]{:S(2)}) async-start(bf16[128,32,128]{0,2,1:T(8,128)(2,1)} %bitcast.16), calls=%async_computation | async-start | bytes 2097152 | tf_op jit(solution)/shard_map/all_to_all | solution.py:44
  24.1 19.5 %all-to-all-start.1 = ((bf16[128,32,128]{0,2,1:T(8,128)(2,1)}), bf16[128,32,128]{0,2,1:T(8,128)(2,1)S(1)}, u32[]{:S(2)}, u32[]{:S(2)}) async-start(bf16[128,32,128]{0,2,1:T(8,128)(2,1)} %bitcast.22), calls=%async_computation.1 | async-start | bytes 2097152 | tf_op jit(solution)/shard_map/all_to_all | solution.py:45
  43.6 19.5 %all-to-all-start.2 = ((bf16[128,32,128]{0,2,1:T(8,128)(2,1)}), bf16[128,32,128]{0,2,1:T(8,128)(2,1)S(1)}, u32[]{:S(2)}, u32[]{:S(2)}) async-start(bf16[128,32,128]{0,2,1:T(8,128)(2,1)} %bitcast.169), calls=%async_computation.2 | async-start | bytes 2097152 | tf_op jit(solution)/shard_map/all_to_all | solution.py:46
  63.1 20.2 %all-to-all-start.3 = ((bf16[128,32,128]{0,2,1:T(8,128)(2,1)}), bf16[128,32,128]{0,2,1:T(8,128)(2,1)}, u32[]{:S(2)}, u32[]{:S(2)}) async-start(bf16[128,32,128]{0,2,1:T(8,128)(2,1)} %bitcast.166), calls=%async_computation.3 | async-start | bytes 2097152 | tf_op jit(solution)/shard_map/all_to_all | solution.py:47
  85.6 6.1 copy-start.9
  125.7 3.5 copy-start.6
  148.1 6.1 copy-start.9
  188.3 3.5 copy-start.6
  210.6 6.1 copy-start.9
  250.8 3.5 copy-start.6
  273.1 6.1 copy-start.9
  313.3 3.5 copy-start.6
  335.6 7.5 %copy-start.13 = (bf16[4,1024,128]{2,1,0:T(8,128)(2,1)S(1)}, bf16[4,1024,128]{2,1,0:T(8,128)(2,1)}, u32[]{:S(2)}) copy-start(bf16[4,1024,128]{2,1,0:T(8,128)(2,1)} %get-tuple-element.59) | copy-start | bytes 3145732
  335.6 26.9 %copy-start.12 = (bf16[4,1024,128]{2,1,0:T(8,128)(2,1)S(1)}, bf16[4,1024,128]{2,1,0:T(8,128)(2,1)}, u32[]{:S(2)}) copy-start(bf16[4,1024,128]{2,1,0:T(8,128)(2,1)} %get-tuple-element.60) | copy-start | bytes 3145732
  338.8 19.5 %all-to-all-start.8 = ((bf16[1024,4,128]{2,1,0:T(4,128)(2,1)}), bf16[1024,4,128]{2,1,0:T(4,128)(2,1)S(1)}, u32[]{:S(2)}, u32[]{:S(2)}) async-start(bf16[1024,4,128]{2,1,0:T(4,128)(2,1)} %bitcast.117), calls=%async_computation.8 | async-start | bytes 2097152 | tf_op jit(solution)/shard_map/all_to_all | solution.py:64
  343.1 38.9 %copy-start.14 = (s32[16]{0:T(128)S(1)}, s32[16]{0:T(128)}, u32[]{:S(2)}) copy-start(s32[16]{0:T(128)} %param.13) | copy-start | bytes 196
  358.2 19.5 %all-to-all-start.4 = ((bf16[1024,4,128]{2,1,0:T(4,128)(2,1)}), bf16[1024,4,128]{2,1,0:T(4,128)(2,1)S(1)}, u32[]{:S(2)}, u32[]{:S(2)}) async-start(bf16[1024,4,128]{2,1,0:T(4,128)(2,1)} %bitcast.120), calls=%async_computation.4 | async-start | bytes 2097152 | tf_op jit(solution)/shard_map/all_to_all | solution.py:61
  377.7 19.5 %all-to-all-start.6 = ((bf16[1024,4,128]{2,1,0:T(4,128)(2,1)}), bf16[1024,4,128]{2,1,0:T(4,128)(2,1)S(1)}, u32[]{:S(2)}, u32[]{:S(2)}) async-start(bf16[1024,4,128]{2,1,0:T(4,128)(2,1)} %bitcast.167), calls=%async_computation.6 | async-start | bytes 2097152 | tf_op jit(solution)/shard_map/all_to_all | solution.py:62
  397.1 20.2 %all-to-all-start.7 = ((bf16[1024,4,128]{2,1,0:T(4,128)(2,1)}), bf16[1024,4,128]{2,1,0:T(4,128)(2,1)}, u32[]{:S(2)}, u32[]{:S(2)}) async-start(bf16[1024,4,128]{2,1,0:T(4,128)(2,1)} %bitcast.168), calls=%async_computation.7 | async-start | bytes 2097152 | tf_op jit(solution)/shard_map/all_to_all | solution.py:63
  417.3 255.4 %all-to-all-start.5 = ((bf16[16,128,4096]{2,1,0:T(8,128)(2,1)}), bf16[16,128,4096]{2,1,0:T(8,128)(2,1)}, u32[]{:S(2)}, u32[]{:S(2)}) async-start(bf16[16,128,4096]{2,1,0:T(8,128)(2,1)} %broadcast_multiply_fusion), calls=%async_computation.5 | async-start | bytes 33554432 | tf_op jit(solution)/shard_map/all_to_all | solution.py:70
  672.7 9.9 %copy-start.1 = (s32[16,8]{0,1:T(8,128)S(1)}, s32[16,8]{0,1:T(8,128)}, u32[]{:S(2)}) copy-start(s32[16,8]{0,1:T(8,128)} %param.12) | copy-start | bytes 1540
  (24 other events, 51.4 us)
where the time goes:
time: 685 us; the launch traced here: 683 us
  waiting for transfers between devices  334 us (49%)
  other arithmetic  130 us (19%)
  matrix products  97.2 us (14%)
  local copies, waits for them, and re-layouts  74.7 us (11%)
  starting transfers between devices  45.3 us (7%)
    all_to_all x1, waiting for transfers between devices, local(): lax.all_to_all(slots, 'dp', split_axis=0, concat_axis=0, tiled=True)  241 us
    dot_general x12, matrix products, forward(): jnp.dot(weight.astype(jnp.bfloat16), va, preferred_element_type=jnp.float32)  53.9 us
    another operation x21, other arithmetic  51.1 us
    dot_general x12, matrix products, forward(): scores = jnp.dot(qa, ka.T, preferred_element_type=jnp.float32) * scale  43.4 us
    mul x4, other arithmetic, forward(): scores = jnp.dot(qa, ka.T, preferred_element_type=jnp.float32) * scale  40.3 us
    another operation x8, other arithmetic, forward(): rest = lax.cumsum(spent, axis=1, reverse=True) - spent  21.7 us
    while x64, local copies, waits for them, and re-layouts  19.8 us
    another operation x8, local copies, waits for them, and re-layouts, forward(): rest = lax.cumsum(spent, axis=1, reverse=True) - spent  19.4 us
  transfers between devices with their start and end apart: 9, of which 9 were waited for; matrix products, arithmetic and copies ran while one was open for 5% of the time, Pallas kernels for 0%

commit v1 on v0

v1 whole, which is shorter than its diff:
```python
import functools

import jax
import jax.numpy as jnp
from jax import lax
from jax.experimental import pallas as pl
from jax.experimental.pallas import tpu as pltpu
from jax.sharding import PartitionSpec as P

HEAD_DIM = 128
LOG2E = 1.4426950408889634
ROWS = 256
NT = (((1,), (1,)), ((), ()))
TN = (((0,), (0,)), ((), ()))


def attention_rows(units, r0, refs, start_ref, tri_ref, dk_acc, dv_acc, outs):
    q_ref, k_ref, v_ref, g_ref = refs
    out_ref, dq_ref = outs
    scale = HEAD_DIM ** (-0.5)
    width = units * 128
    c0 = pl.multiple_of(r0 + ROWS - width, 128)

    def load(ref, first, count):
        return ref[pl.ds(first // 128, count // 128), 0].reshape(count, HEAD_DIM)

    def store(ref, x):
        ref[pl.ds(r0 // 128, ROWS // 128), 0] = x.astype(jnp.bfloat16).reshape(
            ROWS // 128, 128, HEAD_DIM
        )

    q, g = load(q_ref, r0, ROWS), load(g_ref, r0, ROWS)
    k, v = load(k_ref, c0, width), load(v_ref, c0, width)
    start = start_ref[pl.ds(r0, ROWS), :1] - c0
    row = lax.broadcasted_iota(jnp.int32, (ROWS, 1), 0) + (r0 - c0)

    edges = list(range(width, 0, -ROWS)) + [0]
    chunks = [(edges[i + 1], edges[i]) for i in range(len(edges) - 1)]
    carry = jnp.zeros((ROWS, 1), jnp.float32)
    out = jnp.zeros((ROWS, HEAD_DIM), jnp.float32)
    kept = []
    for lo, hi in chunks:
        n = hi - lo
        t = lax.dot_general(q, k[lo:hi], NT, preferred_element_type=jnp.float32) * (scale * LOG2E)
        col = lax.broadcasted_iota(jnp.int32, (ROWS, n), 1) + lo
        t = jnp.where((col >= start) & (col < row), t, -1e30)
        tail = jnp.log2(1.0 + jnp.exp2(-jnp.abs(t)))
        z = jnp.maximum(t, 0.0) + tail
        ls = jnp.minimum(t, 0.0) - tail
        rest = jnp.dot(
            z.astype(jnp.bfloat16), tri_ref[0, :n, :n], preferred_element_type=jnp.float32
        ) + carry
        carry = rest[:, :1] + z[:, :1]
        w = jnp.exp2(ls - rest)
        wb = w.astype(jnp.bfloat16)
        out += jnp.dot(wb, v[lo:hi], preferred_element_type=jnp.float32)
        dv_acc[pl.ds(pl.multiple_of(c0 + lo, 128), n), :] += lax.dot_general(
            wb, g, TN, preferred_element_type=jnp.float32
        )
        dw = lax.dot_general(g, v[lo:hi], NT, preferred_element_type=jnp.float32)
        kept.append((w * dw, jnp.exp2(ls)))
    store(out_ref, out)

    carry = jnp.zeros((ROWS, 1), jnp.float32)
    dq = jnp.zeros((ROWS, HEAD_DIM), jnp.float32)
    for (lo, hi), (a, sig) in reversed(list(zip(chunks, kept))):
        n = hi - lo
        upto = jnp.dot(
            a.astype(jnp.bfloat16), tri_ref[1, :n, :n], preferred_element_type=jnp.float32
        ) + (a + carry)
        carry = upto[:, n - 1 :]
        ds = (a - sig * upto).astype(jnp.bfloat16)
        dq += jnp.dot(ds, k[lo:hi], preferred_element_type=jnp.float32)
        dk_acc[pl.ds(pl.multiple_of(c0 + lo, 128), n), :] += lax.dot_general(
            ds, q, TN, preferred_element_type=jnp.float32
        )
    store(dq_ref, dq * scale)


def attention_kernel(
    units_ref, q_ref, k_ref, v_ref, g_ref, start_ref,
    out_ref, dq_ref, dk_ref, dv_ref, tri_ref, dk_acc, dv_acc,
):
    @pl.when(pl.program_id(0) == 0)
    def _():
        a = lax.broadcasted_iota(jnp.int32, (ROWS, ROWS), 0)
        b = lax.broadcasted_iota(jnp.int32, (ROWS, ROWS), 1)
        tri_ref[0] = jnp.where(a > b, 1.0, 0.0).astype(jnp.bfloat16)
        tri_ref[1] = jnp.where(a < b, 1.0, 0.0).astype(jnp.bfloat16)

    dk_acc[...] = jnp.zeros_like(dk_acc)
    dv_acc[...] = jnp.zeros_like(dv_acc)

    @pl.loop(0, dk_acc.shape[0] // ROWS)
    def _(i):
        r0 = pl.multiple_of(i * ROWS, ROWS)
        units = units_ref[i]
        for n in range(2, 7):
            @pl.when(units == n)
            def _():
                attention_rows(
                    n, r0, (q_ref, k_ref, v_ref, g_ref), start_ref, tri_ref,
                    dk_acc, dv_acc, (out_ref, dq_ref),
                )

    shape = dk_ref.shape
    dk_ref[...] = (dk_acc[...] * HEAD_DIM ** (-0.5)).astype(jnp.bfloat16).reshape(shape)
    dv_ref[...] = dv_acc[...].astype(jnp.bfloat16).reshape(shape)


def attention(x, start, units):
    blocks, _, rows, width = x.shape
    heads = width // HEAD_DIM
    count = blocks * rows
    block = (blocks, 1, rows, HEAD_DIM)
    part = jax.ShapeDtypeStruct((blocks, 1, rows, width), jnp.bfloat16)
    outs = pl.pallas_call(
        attention_kernel,
        out_shape=[part] * 4,
        grid_spec=pltpu.PrefetchScalarGridSpec(
            num_scalar_prefetch=1,
            grid=(heads,),
            in_specs=[
                pl.BlockSpec(block, functools.partial(lambda a, h, u: (0, a, 0, h), a))
                for a in range(4)
            ]
            + [pl.BlockSpec((count, 128), lambda h, u: (0, 0))],
            out_specs=[pl.BlockSpec(block, lambda h, u: (0, 0, 0, h))] * 4,
            scratch_shapes=[
                pltpu.VMEM((2, ROWS, ROWS), jnp.bfloat16),
                pltpu.VMEM((count, HEAD_DIM), jnp.float32),
                pltpu.VMEM((count, HEAD_DIM), jnp.float32),
            ],
        ),
        compiler_params=pltpu.CompilerParams(vmem_limit_bytes=40 * 1024 * 1024),
        cost_estimate=pl.CostEstimate(
            flops=16 * heads * count * count * HEAD_DIM // 2,
            bytes_accessed=8 * count * width * 2,
            transcendentals=2 * heads * count * count,
        ),
    )(units, x, x, x, x, start)
    return outs


def document_starts(lengths, count):
    firsts = jnp.cumsum(lengths) - lengths
    places = jnp.arange(count, dtype=jnp.int32)
    start = jnp.max(jnp.where(firsts[None, :] <= places[:, None], firsts[None, :], 0), axis=1)
    head = start[::ROWS]
    units = (places[::ROWS] + ROWS) // 128 - head // 128
    return jnp.broadcast_to(start[:, None], (count, 128)), jnp.clip(units, 2, 6).astype(jnp.int32)


def local(queries, keys, values, grad_mixed, doc_lengths, owner):
    rows, width = queries.shape
    group = lax.axis_index("dp")
    groups = lax.axis_size("dp")
    peers = lax.axis_size("seq")
    piece = width // peers

    lengths = lax.dynamic_index_in_dim(doc_lengths, group, 0, keepdims=False)
    start, units = document_starts(lengths, rows * peers)

    x = jnp.stack([queries, keys, values, grad_mixed]).reshape(4, rows, peers, piece)
    x = lax.all_to_all(
        jnp.transpose(x, (2, 0, 1, 3)), "seq", split_axis=0, concat_axis=0, tiled=True
    )
    out, dq, dk, dv = attention(x, start, units)

    grads = jnp.concatenate([dq, dk, dv], axis=1)
    grads = lax.all_to_all(grads, "seq", split_axis=0, concat_axis=0, tiled=True)
    grads = jnp.transpose(grads, (1, 2, 0, 3)).reshape(3, rows, width)

    small = rows // groups
    spread = jnp.transpose(out.reshape(peers, groups, small, piece), (1, 0, 2, 3))
    spread = lax.all_to_all(
        spread.reshape(groups * peers, small, piece), ("dp", "seq"),
        split_axis=0, concat_axis=0, tiled=True,
    ).reshape(groups, peers, small, piece)
    sender = jnp.argsort(owner)
    slots = jnp.take(spread, sender, axis=0)
    landed = lax.all_to_all(slots, "dp", split_axis=0, concat_axis=0, tiled=True)
    mixed = jnp.transpose(landed, (0, 2, 1, 3)).reshape(rows, width)
    return (mixed, grads[0], grads[1], grads[2])


def solution(mesh):
    placed = P(("dp", "seq"), None)
    return jax.shard_map(
        local,
        mesh=mesh,
        in_specs=(placed,) * 4 + (P(), P()),
        out_specs=(placed,) * 4,
        check_vma=False,
    )
```

time: 685 us -> 206 us (0.30)
  waiting for transfers between devices: 334 us -> 117 us
  other arithmetic: 130 us -> 9.37 us
  matrix products: 97.2 us -> 0 us
  local copies, waits for them, and re-layouts: 74.7 us -> 24.7 us
  Pallas kernels: 0 us -> 27.7 us
  starting transfers between devices: 45.3 us -> 26.6 us
    all_to_all x1, waiting for transfers between devices: 241 us -> 13.7 us  [local(): lax.all_to_all(slots, 'dp', split_axis=0, concat_axis=0, tiled=True)]
    dot_general x24 -> x0, matrix products: 97.2 us -> none  [the longest x12 53.9 us: forward(): jnp.dot(weight.astype(jnp.bfloat16), va, preferred_element_type=jnp.float32)]
    another operation x29 -> x1, other arithmetic: 72.8 us -> 0.03 us
    mul x5 -> x0, other arithmetic: 46.2 us -> none  [the longest x4 40.3 us: forward(): scores = jnp.dot(qa, ka.T, preferred_element_type=jnp.float32) * scale]
    while x68 -> x0, local copies, waits for them, and re-layouts: 29.5 us -> none
    pallas_call x0 -> x1, Pallas kernels: none -> 27.7 us  [attention(): pl.pallas_call(attention_kernel, out_shape=[part] * 4, grid_spec=pltpu.Pr...]
    another operation x24 -> x4, local copies, waits for them, and re-layouts: 19.5 us -> 3.69 us  [local(): jnp.stack([queries, keys, values, grad_mixed])]
    all_to_all x8 -> x3, starting transfers between devices: 37.6 us -> 22.2 us  [the longest x1 9.69 us: local(): lax.all_to_all(spread.reshape(groups * peers, small, piece), ('dp', 'seq'...]
  transfers between devices with their start and end apart: 9 -> 4, of which waited for: 9 -> 4; matrix products, arithmetic and copies ran while one was open for 5% -> 2% of each run, Pallas kernels for 0% -> 0%
where the time goes in v1:
time: 206 us
  waiting for transfers between devices  117 us (57%)
  Pallas kernels  27.7 us (13%)
  starting transfers between devices  26.6 us (13%)
  local copies, waits for them, and re-layouts  24.7 us (12%)
  other arithmetic  9.37 us (5%)
    all_to_all x1, waiting for transfers between devices, local(): lax.all_to_all(jnp.transpose(x, (2, 0, 1, 3)), 'seq', split_axis=0, conca...  48.3 us
    all_to_all x1, waiting for transfers between devices, local(): lax.all_to_all(grads, 'seq', split_axis=0, concat_axis=0, tiled=True)  37.6 us
    pallas_call x1, Pallas kernels, attention(): pl.pallas_call(attention_kernel, out_shape=[part] * 4, grid_spec=pltpu.Pr...  27.7 us
    all_to_all x1, waiting for transfers between devices, local(): lax.all_to_all(spread.reshape(groups * peers, small, piece), ('dp', 'seq'...  17.3 us
    all_to_all x1, waiting for transfers between devices, local(): lax.all_to_all(slots, 'dp', split_axis=0, concat_axis=0, tiled=True)  13.7 us
    unnamed x18, local copies, waits for them, and re-layouts  11.8 us
    all_to_all x1, starting transfers between devices, local(): lax.all_to_all(spread.reshape(groups * peers, small, piece), ('dp', 'seq'...  9.69 us
    all_to_all x1, starting transfers between devices, local(): lax.all_to_all(grads, 'seq', split_axis=0, concat_axis=0, tiled=True)  6.42 us
  transfers between devices with their start and end apart: 4, of which 4 were waited for; matrix products, arithmetic and copies ran while one was open for 2% of the time, Pallas kernels for 0%

profile of v1, /device:TPU:1, one launch (start us, length us, event | category | flops | bytes accessed | tf_op | source)
XLA Modules:
  0.0 206.0 jit_solution(10151988712185060237)
XLA Ops:
  0.6 1.7 copy.28
  4.1 1.6 copy.26
  5.7 1.3 copy.30
  7.0 1.6 copy.25
  8.7 1.3 copy.29
  10.0 3.4 %maximum_bitcast_fusion = bf16[8,4,128,512]{3,2,1,0:T(8,128)(2,1)} fusion(bf16[1,128,8,512]{3,1,0,2:T(8,128)(2,1)S(1)} %copy.32, bf16[1,128,8,512]{3,1,0,2:T(8,128)(2,1)S(1)} %copy.31, bf16[1,128,8,512]{3,1,0,2:T(8,128)(2,1)} %copy.30, bf16[1,128,8,512]{3,1,0,2:T(8,128)(2,1)} %copy.29), kind=kLoop, calls=%fused_computation.1 | loop fusion | flops 6291456 | bytes 8388608 | tf_op jit(solution)/shard_map/transpose | solution.py:166
  13.4 6.1 %all-to-all-start = ((bf16[8,4,128,512]{3,2,1,0:T(8,128)(2,1)}), bf16[8,4,128,512]{3,2,1,0:T(8,128)(2,1)}, u32[]{:S(2)}, u32[]{:S(2)}) async-start(bf16[8,4,128,512]{3,2,1,0:T(8,128)(2,1)} %maximum_bitcast_fusion), calls=%async_computation | async-start | bytes 8388608 | tf_op jit(solution)/shard_map/all_to_all | solution.py:165
  20.1 48.3 %all-to-all-done.q_ref.k_ref.v_ref.g_ref = bf16[8,4,128,512]{3,2,1,0:T(8,128)(2,1)} async-done(((bf16[8,4,128,512]{3,2,1,0:T(8,128)(2,1)}), bf16[8,4,128,512]{3,2,1,0:T(8,128)(2,1)}, u32[]{:S(2)}, u32[]{:S(2)}) %all-to-all-start) | async-done | bytes 4194336 | tf_op jit(solution)/shard_map/all_to_all | solution.py:165
  68.6 27.7 %shard_map.93 = (bf16[8,1,128,512]{3,2,1,0:T(8,128)(2,1)S(1)}, bf16[8,1,128,512]{3,2,1,0:T(8,128)(2,1)S(1)}, bf16[8,1,128,512]{3,2,1,0:T(8,128)(2,1)S(1)}, bf16[8,1,128,512]{3,2,1,0:T(8,128)(2,1)S(1)}) custom-call(s32[4]{0:T(128)S(1)} %subtract_clamp_fusion.units_ref, bf16[8,4,128,512]{3,2,1,0:T(8,128)(2,1)} %all-to-all-done.q_ref.k_ref.v_ref.g_ref, ...), custom_call_target="tpu_custom_call" | custom-call | flops 4294967296 | bytes 8388608 | tf_op jit(solution)/shard_map/pallas_call | solution.py:117
  97.4 9.7 %all-to-all-start.1 = ((bf16[128,8,512]{2,1,0:T(8,128)(2,1)}), bf16[128,8,512]{2,1,0:T(8,128)(2,1)}, u32[]{:S(2)}, u32[]{:S(2)}) async-start(bf16[128,8,512]{2,1,0:T(8,128)(2,1)} %bitcast.20), calls=%async_computation.1 | async-start | bytes 2097152 | tf_op jit(solution)/shard_map/all_to_all | solution.py:176
  108.4 17.3 %all-to-all-done.1 = bf16[128,8,512]{2,1,0:T(8,128)(2,1)} async-done(((bf16[128,8,512]{2,1,0:T(8,128)(2,1)}), bf16[128,8,512]{2,1,0:T(8,128)(2,1)}, u32[]{:S(2)}, u32[]{:S(2)}) %all-to-all-start.1) | async-done | bytes 1048608 | tf_op jit(solution)/shard_map/all_to_all | solution.py:176
  125.7 2.8 %gather_fusion = bf16[16,8,8,512]{3,2,1,0:T(8,128)(2,1)} fusion(bf16[16,8,8,512]{3,2,1,0:T(8,128)(2,1)} %bitcast.8, s32[1024]{0:T(1024)S(1)} %pad_clamp_fusion), kind=kCustom, calls=%fused_computation | custom fusion | bytes 2097216 | tf_op jit(solution)/shard_map/jit(_take)/gather | solution.py:181
  128.5 2.4 %broadcast_select_fusion = bf16[16,8,8,512]{3,2,1,0:T(8,128)(2,1)} fusion(bf16[16,8,8,512]{3,2,1,0:T(8,128)(2,1)} %gather_fusion, pred[16]{0:T(512)(128)(4,1)S(1)} %compare_and_fusion), kind=kLoop, calls=%fused_computation.3 | loop fusion | flops 524288 | bytes 2097168 | tf_op jit(solution)/shard_map/jit(_take)/select_n | solution.py:181
  130.8 4.3 %all-to-all-start.2 = ((bf16[16,8,8,512]{3,2,1,0:T(8,128)(2,1)}), bf16[16,8,8,512]{3,2,1,0:T(8,128)(2,1)}, u32[]{:S(2)}, u32[]{:S(2)}) async-start(bf16[16,8,8,512]{3,2,1,0:T(8,128)(2,1)} %broadcast_select_fusion), calls=%async_computation.2 | async-start | bytes 2097152 | tf_op jit(solution)/shard_map/all_to_all | solution.py:182
  135.2 2.0 pad_maximum_fusion
  137.2 13.7 %all-to-all-done.2 = bf16[16,8,8,512]{3,2,1,0:T(8,128)(2,1)} async-done(((bf16[16,8,8,512]{3,2,1,0:T(8,128)(2,1)}), bf16[16,8,8,512]{3,2,1,0:T(8,128)(2,1)}, u32[]{:S(2)}, u32[]{:S(2)}) %all-to-all-start.2) | async-done | bytes 1048608 | tf_op jit(solution)/shard_map/all_to_all | solution.py:182
  150.9 6.4 %all-to-all-start.3 = ((bf16[8,3,128,512]{3,2,1,0:T(8,128)(2,1)}), bf16[8,3,128,512]{3,2,1,0:T(8,128)(2,1)S(1)}, u32[]{:S(2)}, u32[]{:S(2)}) async-start(bf16[8,3,128,512]{3,2,1,0:T(8,128)(2,1)} %pad_maximum_fusion), calls=%async_computation.3 | async-start | bytes 6291456 | tf_op jit(solution)/shard_map/all_to_all | solution.py:171
  157.3 37.6 %all-to-all-done.3 = bf16[8,3,128,512]{3,2,1,0:T(8,128)(2,1)S(1)} async-done(((bf16[8,3,128,512]{3,2,1,0:T(8,128)(2,1)}), bf16[8,3,128,512]{3,2,1,0:T(8,128)(2,1)S(1)}, u32[]{:S(2)}, u32[]{:S(2)}) %all-to-all-start.3) | async-done | bytes 3145760 | tf_op jit(solution)/shard_map/all_to_all | solution.py:171
  194.9 1.8 fusion
  196.6 1.8 copy.34
  198.4 1.3 copy.37
  200.4 1.3 copy.38
  202.4 1.3 copy.39
  203.7 2.3 %copy.41 = bf16[128,4096]{1,0:T(8,128)(2,1)} copy(bf16[128,4096]{1,0:T(8,128)(2,1)} %bitcast.10) | data formatting | bytes 2097152
  (30 shorter events, 6.2 us)
Async XLA Ops:
  0.6 2.3 %copy-start.2 = (bf16[128,4096]{1,0:T(8,128)(2,1)S(1)}, bf16[128,4096]{1,0:T(8,128)(2,1)}, u32[]{:S(2)}) copy-start(bf16[128,4096]{1,0:T(8,128)(2,1)} %param.8) | copy-start | bytes 3145732
  13.4 6.1 %copy-start.3 = (s32[16,8]{0,1:T(8,128)S(1)}, s32[16,8]{0,1:T(8,128)}, u32[]{:S(2)}) copy-start(s32[16,8]{0,1:T(8,128)} %param.10) | copy-start | bytes 1540
  13.4 55.0 %all-to-all-start = ((bf16[8,4,128,512]{3,2,1,0:T(8,128)(2,1)}), bf16[8,4,128,512]{3,2,1,0:T(8,128)(2,1)}, u32[]{:S(2)}, u32[]{:S(2)}) async-start(bf16[8,4,128,512]{3,2,1,0:T(8,128)(2,1)} %maximum_bitcast_fusion), calls=%async_computation | async-start | bytes 8388608 | tf_op jit(solution)/shard_map/all_to_all | solution.py:165
  96.3 10.8 %copy-start.4 = (s32[16]{0:T(128)S(1)}, s32[16]{0:T(128)}, u32[]{:S(2)}) copy-start(s32[16]{0:T(128)} %param.11) | copy-start | bytes 196
  97.4 28.2 %all-to-all-start.1 = ((bf16[128,8,512]{2,1,0:T(8,128)(2,1)}), bf16[128,8,512]{2,1,0:T(8,128)(2,1)}, u32[]{:S(2)}, u32[]{:S(2)}) async-start(bf16[128,8,512]{2,1,0:T(8,128)(2,1)} %bitcast.20), calls=%async_computation.1 | async-start | bytes 2097152 | tf_op jit(solution)/shard_map/all_to_all | solution.py:176
  130.8 20.0 %all-to-all-start.2 = ((bf16[16,8,8,512]{3,2,1,0:T(8,128)(2,1)}), bf16[16,8,8,512]{3,2,1,0:T(8,128)(2,1)}, u32[]{:S(2)}, u32[]{:S(2)}) async-start(bf16[16,8,8,512]{3,2,1,0:T(8,128)(2,1)} %broadcast_select_fusion), calls=%async_computation.2 | async-start | bytes 2097152 | tf_op jit(solution)/shard_map/all_to_all | solution.py:182
  150.9 44.0 %all-to-all-start.3 = ((bf16[8,3,128,512]{3,2,1,0:T(8,128)(2,1)}), bf16[8,3,128,512]{3,2,1,0:T(8,128)(2,1)S(1)}, u32[]{:S(2)}, u32[]{:S(2)}) async-start(bf16[8,3,128,512]{3,2,1,0:T(8,128)(2,1)} %pad_maximum_fusion), calls=%async_computation.3 | async-start | bytes 6291456 | tf_op jit(solution)/shard_map/all_to_all | solution.py:171
  196.6 3.1 %copy-start.1 = (bf16[1,128,8,512]{3,1,0,2:T(8,128)(2,1)S(1)}, bf16[1,128,8,512]{3,1,0,2:T(8,128)(2,1)}, u32[]{:S(2)}) copy-start(bf16[1,128,8,512]{3,1,0,2:T(8,128)(2,1)} %get-tuple-element.23) | copy-start | bytes 3145732
  196.6 5.1 %copy-start = (bf16[1,128,8,512]{3,1,0,2:T(8,128)(2,1)S(1)}, bf16[1,128,8,512]{3,1,0,2:T(8,128)(2,1)}, u32[]{:S(2)}) copy-start(bf16[1,128,8,512]{3,1,0,2:T(8,128)(2,1)} %get-tuple-element.22) | copy-start | bytes 3145732
